TPU v7x, 128 devices: a whole 4x4x4 slice. The times are simulated.
128 devices in a mesh: rep: 8 (over x, core), ctx: 16 (over y, z).
Axes of the slice: x: 4, y: 4, z: 4, core: 2. Of those that a mesh axis runs over, the one named last changes fastest.
Arguments:
- queries: bfloat16 [8, 16384, 512], P('rep', 'ctx'), may hold values from -6 to 6
- key_states: bfloat16 [8, 16384, 512], P('rep', 'ctx'), may hold values from -6 to 6
- value_states: bfloat16 [8, 16384, 512], P('rep', 'ctx'), may hold values from -6 to 6
- grad_out: bfloat16 [8, 16384, 1024], P('rep', 'ctx'), may hold values from -6 to 6
- out_weight: bfloat16 [512, 1024], replicated, may hold values from -0.25 to 0.25
Outputs:
- outputs: bfloat16 [8, 16384, 1024], P('rep', 'ctx')
- grad_queries: bfloat16 [8, 16384, 512], P('rep', 'ctx')
- grad_keys: bfloat16 [8, 16384, 512], P('rep', 'ctx')
- grad_values: bfloat16 [8, 16384, 512], P('rep', 'ctx')
- grad_weight: float32 [512, 1024], P('ctx', 'rep')
All inputs are finite; a program needn't handle non-finite values.
Results may differ from a plain program's by a relative error of at most 0.012.
Values may be sent and summed in bfloat16 or wider, within the bound.
No kernel may reach another device: no remote copies, remote signals or barrier semaphores. Data moves between devices by JAX's collectives and lax.ppermute only.
A program may use at most 320 MiB of HBM per device.

v0:
```python
from functools import reduce

import jax
import jax.numpy as jnp
from jax import lax
from jax.sharding import PartitionSpec as P

HEADS = 8
HDIM = 64


SCALE = 0.125


def partner(value, axis, stride):
    mask = 2**stride
    pairs = [(source, source ^ mask) for source in range(lax.axis_size(axis))]
    return lax.ppermute(value, axis, pairs)


def pool_pairs(matrix):
    paired = matrix.astype(jnp.float32).reshape(matrix.shape[0] // 2, 2, matrix.shape[1])
    return (0.5 * (paired[:, 0] + paired[:, 1])).astype(jnp.bfloat16)


def spread_rows(parent):
    return jnp.repeat(parent, 2, axis=0) * 0.5


def split_heads(matrix, group_heads):
    return matrix.reshape(matrix.shape[0], group_heads, matrix.shape[1] // group_heads)


def head_scores(query_heads, key_heads):
    return (
        jnp.einsum("phd,rhd->hpr", query_heads, key_heads, preferred_element_type=jnp.float32)
        * SCALE
    )


def widened(stat, head_dim):
    return jnp.repeat(stat.T, head_dim, axis=1)


def attend_forward(query_rows, key_rows, value_rows, group_heads):
    scores = head_scores(split_heads(query_rows, group_heads), split_heads(key_rows, group_heads))
    row_max = jnp.max(scores, axis=2)
    exponent = jnp.exp(scores - row_max[:, :, None])
    totals = jnp.sum(exponent, axis=2)
    weighted = jnp.einsum(
        "hpr,rhd->phd",
        exponent.astype(jnp.bfloat16),
        split_heads(value_rows, group_heads),
        preferred_element_type=jnp.float32,
    )
    return (row_max, totals, weighted.reshape(query_rows.shape[0], -1))


def attend_backward(query_rows, key_rows, value_rows, row_max, grad_rows, grad_scale, group_heads):
    query_heads = split_heads(query_rows, group_heads)
    key_heads = split_heads(key_rows, group_heads)
    value_heads = split_heads(value_rows, group_heads)
    grad_heads = split_heads(grad_rows, group_heads)
    exponent = jnp.exp(head_scores(query_heads, key_heads) - row_max[:, :, None])
    grad_prob = jnp.einsum(
        "phd,rhd->hpr", grad_heads, value_heads, preferred_element_type=jnp.float32
    )
    grad_score = (exponent * (grad_prob - grad_scale[:, :, None])).astype(jnp.bfloat16)
    grad_query = SCALE * jnp.einsum(
        "hpr,rhd->phd", grad_score, key_heads, preferred_element_type=jnp.float32
    )
    grad_key = SCALE * jnp.einsum(
        "hpr,phd->rhd", grad_score, query_heads, preferred_element_type=jnp.float32
    )
    grad_value = jnp.einsum(
        "hpr,phd->rhd",
        exponent.astype(jnp.bfloat16),
        grad_heads,
        preferred_element_type=jnp.float32,
    )
    return (
        grad_query.reshape(query_rows.shape[0], -1),
        grad_key.reshape(key_rows.shape[0], -1),
        grad_value.reshape(key_rows.shape[0], -1),
    )


def on_device(queries, key_states, value_states, grad_out, out_weight):
    query_block = queries[0]
    key_block = key_states[0]
    value_block = value_states[0]
    grad_rows_all = grad_out[0]
    ctx_count = lax.axis_size("ctx")
    levels = ctx_count.bit_length() - 1
    device_index = lax.axis_index("ctx")
    fine_rows = query_block.shape[0]
    query_pyramid = [query_block]
    for level_id in range(1, levels):
        query_pyramid.append(pool_pairs(query_pyramid[-1]))
    held_keys = key_block
    held_values = value_block
    remote_keys = []
    remote_values = []
    for level_id in range(levels):
        far_keys, far_values = partner((held_keys, held_values), "ctx", level_id)
        remote_keys.append(far_keys)
        remote_values.append(far_values)
        if level_id + 1 < levels:
            upper_side = device_index // 2**level_id % 2 == 1
            near_keys = pool_pairs(held_keys)
            near_values = pool_pairs(held_values)
            coarse_far_keys = pool_pairs(far_keys)
            coarse_far_values = pool_pairs(far_values)
            held_keys = jnp.where(
                upper_side,
                jnp.concatenate([coarse_far_keys, near_keys], 0),
                jnp.concatenate([near_keys, coarse_far_keys], 0),
            )
            held_values = jnp.where(
                upper_side,
                jnp.concatenate([coarse_far_values, near_values], 0),
                jnp.concatenate([near_values, coarse_far_values], 0),
            )
    grad_attn = lax.dot_general(
        grad_rows_all, out_weight, (((1,), (1,)), ((), ())), preferred_element_type=jnp.float32
    ).astype(jnp.bfloat16)
    group_heads = min(HEADS, max(1, 128 // HDIM))
    group_width = group_heads * HDIM
    group_count = HEADS // group_heads
    selector = (
        jnp.arange(group_width)[:, None] // HDIM == jnp.arange(group_heads)[None, :]
    ).astype(jnp.float32)

    def group_pass(head_group):
        first_col = head_group * group_width

        def columns_of(matrix):
            return matrix[:, first_col : first_col + group_width]

        grad_rows = columns_of(grad_attn)
        operands = []
        maxima = []
        row_totals = []
        products = []
        for level_id in range(levels):
            repeat_by = 2**level_id
            query_rows = columns_of(query_pyramid[level_id])
            if level_id == 0:
                key_rows = jnp.concatenate([columns_of(key_block), columns_of(remote_keys[0])], 0)
                value_rows = jnp.concatenate(
                    [columns_of(value_block), columns_of(remote_values[0])], 0
                )
            else:
                key_rows = columns_of(remote_keys[level_id])
                value_rows = columns_of(remote_values[level_id])
            row_max, totals, weighted = attend_forward(
                query_rows, key_rows, value_rows, group_heads
            )
            operands.append((query_rows, key_rows, value_rows, row_max))
            maxima.append(jnp.repeat(row_max, repeat_by, axis=1))
            row_totals.append(jnp.repeat(totals, repeat_by, axis=1))
            products.append(jnp.repeat(weighted, repeat_by, axis=0))
        joint_max = reduce(jnp.maximum, maxima)
        factors = [
            2.0**level_id * jnp.exp(maxima[level_id] - joint_max) for level_id in range(levels)
        ]
        totals_all = factors[0] * row_totals[0]
        combined = widened(factors[0], HDIM) * products[0]
        for level_id in range(1, levels):
            totals_all = totals_all + factors[level_id] * row_totals[level_id]
            combined = combined + widened(factors[level_id], HDIM) * products[level_id]
        attn_rows = (combined / widened(totals_all, HDIM)).astype(jnp.bfloat16)
        grad_wide = grad_rows.astype(jnp.float32)
        row_delta = jnp.dot(
            grad_wide * attn_rows.astype(jnp.float32), selector, precision=lax.Precision.HIGHEST
        ).T
        grad_query = jnp.zeros((fine_rows, group_width), jnp.float32)
        far_grad_keys = []
        far_grad_values = []
        own_key_grad = grad_query
        own_value_grad = grad_query
        for level_id in range(levels):
            repeat_by = 2**level_id
            coarse_rows = fine_rows // repeat_by
            row_share = factors[level_id] / totals_all
            grad_level = (widened(row_share, HDIM) * grad_wide).reshape(
                coarse_rows, repeat_by, group_width
            )
            grad_level = grad_level.sum(axis=1).astype(jnp.bfloat16)
            grad_scale = (
                (row_share * row_delta).reshape(group_heads, coarse_rows, repeat_by).sum(axis=2)
            )
            query_rows, key_rows, value_rows, row_max = operands[level_id]
            part_query, part_key, part_value = attend_backward(
                query_rows, key_rows, value_rows, row_max, grad_level, grad_scale, group_heads
            )
            grad_query = grad_query + jnp.repeat(part_query, repeat_by, axis=0) / repeat_by
            if level_id == 0:
                own_key_grad = part_key[:fine_rows]
                own_value_grad = part_value[:fine_rows]
                far_grad_keys.append(part_key[fine_rows:])
                far_grad_values.append(part_value[fine_rows:])
            else:
                far_grad_keys.append(part_key)
                far_grad_values.append(part_value)
        return (attn_rows, grad_query, own_key_grad, own_value_grad, far_grad_keys, far_grad_values)

    results = [group_pass(head_group) for head_group in range(group_count)]

    def joined(position):
        return jnp.concatenate([result[position] for result in results], 1)

    def joined_level(position, level_id):
        return jnp.concatenate([result[position][level_id] for result in results], 1)

    attn_all = joined(0)
    grad_query_all = joined(1)
    own_key_grads = joined(2)
    own_value_grads = joined(3)
    sibling_key_grads = [joined_level(4, level_id) for level_id in range(levels)]
    sibling_value_grads = [joined_level(5, level_id) for level_id in range(levels)]
    outputs = jnp.dot(attn_all, out_weight, preferred_element_type=jnp.float32).astype(jnp.bfloat16)
    pending_keys = None
    pending_values = None
    for level_id in reversed(range(levels)):
        outgoing_keys = sibling_key_grads[level_id]
        outgoing_values = sibling_value_grads[level_id]
        retained_keys = None
        retained_values = None
        if pending_keys is not None:
            half_rows = pending_keys.shape[0] // 2
            upper_side = device_index // 2**level_id % 2 == 1
            low_keys = spread_rows(pending_keys[:half_rows])
            high_keys = spread_rows(pending_keys[half_rows:])
            low_values = spread_rows(pending_values[:half_rows])
            high_values = spread_rows(pending_values[half_rows:])
            retained_keys = jnp.where(upper_side, high_keys, low_keys)
            retained_values = jnp.where(upper_side, high_values, low_values)
            outgoing_keys = outgoing_keys + jnp.where(upper_side, low_keys, high_keys)
            outgoing_values = outgoing_values + jnp.where(upper_side, low_values, high_values)
        incoming_keys, incoming_values = partner((outgoing_keys, outgoing_values), "ctx", level_id)
        if retained_keys is None:
            pending_keys = incoming_keys
            pending_values = incoming_values
        else:
            pending_keys = retained_keys + incoming_keys
            pending_values = retained_values + incoming_values
    grad_keys = (pending_keys + own_key_grads).astype(jnp.bfloat16)
    grad_values = (pending_values + own_value_grads).astype(jnp.bfloat16)
    partial_rows = lax.psum_scatter(
        lax.dot_general(
            attn_all, grad_rows_all, (((0,), (0,)), ((), ())), preferred_element_type=jnp.float32
        ),
        "ctx",
        scatter_dimension=0,
        tiled=True,
    )
    grad_weight = lax.psum_scatter(partial_rows, "rep", scatter_dimension=1, tiled=True)
    return (
        outputs[None],
        grad_query_all.astype(jnp.bfloat16)[None],
        grad_keys[None],
        grad_values[None],
        grad_weight,
    )


def solution(mesh):
    placed = (
        P("rep", "ctx", None),
        P("rep", "ctx", None),
        P("rep", "ctx", None),
        P("rep", "ctx", None),
        P(),
    )
    return jax.shard_map(
        on_device,
        mesh=mesh,
        in_specs=placed,
        out_specs=(
            P("rep", "ctx", None),
            P("rep", "ctx", None),
            P("rep", "ctx", None),
            P("rep", "ctx", None),
            P("ctx", "rep"),
        ),
        check_vma=False,
    )
```

profile of v0, /device:TPU:0, one launch (start us, length us, event | category | flops | bytes accessed | tf_op | source)
XLA Modules:
  0.0 1136.5 jit_solution(15909025547008104438)
XLA Ops:
  23.8 9.0 convert_reduce_fusion
  119.4 9.4 bitcast_reduce_fusion.3
  128.8 9.1 fusion.4
  138.0 8.2 bitcast_reduce_fusion.2
  146.1 9.2 fusion.6
  155.3 8.4 bitcast_reduce_fusion.1
  163.7 9.1 fusion.8
  172.8 8.1 bitcast_reduce_fusion
  180.9 9.2 fusion.10
  383.9 9.7 fusion.52
  420.1 9.8 fusion.51
  457.8 9.7 fusion.50
  495.3 9.6 fusion.49
  650.0 7.6 convolution_bitcast_fusion.3
  659.8 7.5 convolution_bitcast_fusion.2
  669.5 7.4 convolution_bitcast_fusion.1
  679.0 7.4 convolution_bitcast_fusion
  760.8 10.3 multiply_convert_fusion.3
  771.1 7.9 fusion.23
  796.2 10.3 multiply_convert_fusion.1
  806.6 7.9 fusion.21
  923.3 19.7 %collective-permute-done.9 = f32[1024,512]{1,0:T(8,128)} collective-permute-done((f32[1024,512]{1,0:T(8,128)}, f32[1024,512]{1,0:T(8,128)}, u32[]{:S(2)}, u32[]{:S(2)}) %collective-permute-start.9) | collective-permute-done | bytes 2097184 | tf_op jit(solution)/shard_map/ppermute | solution.py:18
  1068.1 18.2 %collective-permute-done.15 = f32[1024,512]{1,0:T(8,128)} collective-permute-done((f32[1024,512]{1,0:T(8,128)}, f32[1024,512]{1,0:T(8,128)}, u32[]{:S(2)}, u32[]{:S(2)}) %collective-permute-start.15) | collective-permute-done | bytes 2097184 | tf_op jit(solution)/shard_map/ppermute | solution.py:18
  1090.6 35.4 %collective-permute-done.11 = f32[1024,512]{1,0:T(8,128)} collective-permute-done((f32[1024,512]{1,0:T(8,128)}, f32[1024,512]{1,0:T(8,128)}, u32[]{:S(2)}, u32[]{:S(2)}) %collective-permute-start.11) | collective-permute-done | bytes 2097184 | tf_op jit(solution)/shard_map/ppermute | solution.py:18
  (1225 shorter events, 859.8 us)
Async XLA Ops:
  7.2 63.7 %copy-start = (bf16[1,1024,1024]{2,1,0:T(8,128)(2,1)S(1)}, bf16[1,1024,1024]{2,1,0:T(8,128)(2,1)}, u32[]{:S(2)}) copy-start(bf16[1,1024,1024]{2,1,0:T(8,128)(2,1)} %param.8) | copy-start | bytes 6291460
  7.2 1054.5 %reduce-scatter.3.cloned.1.call-start = ((), (), s32[]{:S(2)}) async-start(), calls=%async_computation.2 | async-start | bytes 2228224 | tf_op jit(solution)/shard_map/reduce_scatter | solution.py:250
  7.2 70.6 %collective-permute-start.4 = (bf16[1024,512]{1,0:T(8,128)(2,1)}, bf16[1024,512]{1,0:T(8,128)(2,1)}, u32[]{:S(2)}, u32[]{:S(2)}) collective-permute-start(bf16[1024,512]{1,0:T(8,128)(2,1)} %bitcast.760), channel_id=1, source_target_pairs={{0,1},{1,0},{2,3},{3,2},{4,5},{5,4},{6,7},{7,6},{8,9},{9,8},{10,11... | collective-permute-start | bytes 3145736 | tf_op jit(solution)/shard_map/ppermute | solution.py:18
  9.3 84.7 %collective-permute-start = (bf16[1024,512]{1,0:T(8,128)(2,1)}, bf16[1024,512]{1,0:T(8,128)(2,1)}, u32[]{:S(2)}, u32[]{:S(2)}) collective-permute-start(bf16[1024,512]{1,0:T(8,128)(2,1)} %bitcast.762), channel_id=1, source_target_pairs={{0,1},{1,0},{2,3},{3,2},{4,5},{5,4},{6,7},{7,6},{8,9},{9,8},{10,11... | collective-permute-start | bytes 3145736 | tf_op jit(solution)/shard_map/ppermute | solution.py:18
  64.2 190.6 %copy-start.156 = (bf16[512,128]{0,1:T(8,128)(2,1)}, bf16[512,128]{0,1:T(8,128)(2,1)S(1)}, u32[]{:S(2)}) copy-start(bf16[512,128]{0,1:T(8,128)(2,1)S(1)} %copy.1512) | copy-start | bytes 393220
  70.8 102.0 %copy-start.70 = (bf16[1024,128]{0,1:T(8,128)(2,1)}, bf16[1024,128]{0,1:T(8,128)(2,1)S(1)}, u32[]{:S(2)}) copy-start(bf16[1024,128]{0,1:T(8,128)(2,1)S(1)} %copy.1532) | copy-start | bytes 786436
  86.7 113.5 %collective-permute-start.5 = (bf16[1024,512]{1,0:T(8,128)(2,1)}, bf16[1024,512]{1,0:T(8,128)(2,1)}, u32[]{:S(2)}, u32[]{:S(2)}) collective-permute-start(bf16[1024,512]{1,0:T(8,128)(2,1)} %maximum_select_fusion.3), channel_id=1, source_target_pairs={{0,2},{1,3},{2,0},{3,1},{4,6},{5,7},{6,4},{7,5},{8,10},{9,11},{10,... | collective-permute-start | bytes 3145736 | tf_op jit(solution)/shard_map/ppermute | solution.py:18
  102.9 109.1 %collective-permute-start.1 = (bf16[1024,512]{1,0:T(8,128)(2,1)}, bf16[1024,512]{1,0:T(8,128)(2,1)}, u32[]{:S(2)}, u32[]{:S(2)}) collective-permute-start(bf16[1024,512]{1,0:T(8,128)(2,1)} %maximum_select_fusion), channel_id=1, source_target_pairs={{0,2},{1,3},{2,0},{3,1},{4,6},{5,7},{6,4},{7,5},{8,10},{9,11},{10,... | collective-permute-start | bytes 3145736 | tf_op jit(solution)/shard_map/ppermute | solution.py:18
  208.0 94.2 %collective-permute-start.6 = (bf16[1024,512]{1,0:T(8,128)(2,1)S(1)}, bf16[1024,512]{1,0:T(8,128)(2,1)}, u32[]{:S(2)}, u32[]{:S(2)}) collective-permute-start(bf16[1024,512]{1,0:T(8,128)(2,1)S(1)} %maximum_select_fusion.4), channel_id=1, source_target_pairs={{0,4},{1,5},{2,6},{3,7},{4,0},{5,1},{6,2},{7,3},{8,12},{9,13},{10,... | collective-permute-start | bytes 3145736 | tf_op jit(solution)/shard_map/ppermute | solution.py:18
  220.7 93.4 %collective-permute-start.2 = (bf16[1024,512]{1,0:T(8,128)(2,1)}, bf16[1024,512]{1,0:T(8,128)(2,1)}, u32[]{:S(2)}, u32[]{:S(2)}) collective-permute-start(bf16[1024,512]{1,0:T(8,128)(2,1)} %maximum_select_fusion.1), channel_id=1, source_target_pairs={{0,4},{1,5},{2,6},{3,7},{4,0},{5,1},{6,2},{7,3},{8,12},{9,13},{10,... | collective-permute-start | bytes 3145736 | tf_op jit(solution)/shard_map/ppermute | solution.py:18
  310.9 58.1 %collective-permute-start.7 = (bf16[1024,512]{1,0:T(8,128)(2,1)}, bf16[1024,512]{1,0:T(8,128)(2,1)}, u32[]{:S(2)}, u32[]{:S(2)}) collective-permute-start(bf16[1024,512]{1,0:T(8,128)(2,1)} %maximum_select_fusion.5), channel_id=1, source_target_pairs={{0,8},{1,9},{2,10},{3,11},{4,12},{5,13},{6,14},{7,15},{8,0},{9,1},... | collective-permute-start | bytes 3145736 | tf_op jit(solution)/shard_map/ppermute | solution.py:18
  340.2 32.8 %collective-permute-start.3 = (bf16[1024,512]{1,0:T(8,128)(2,1)}, bf16[1024,512]{1,0:T(8,128)(2,1)S(1)}, u32[]{:S(2)}, u32[]{:S(2)}) collective-permute-start(bf16[1024,512]{1,0:T(8,128)(2,1)} %maximum_select_fusion.2), channel_id=1, source_target_pairs={{0,8},{1,9},{2,10},{3,11},{4,12},{5,13},{6,14},{7,15},{8,0},{9,1},... | collective-permute-start | bytes 3145736 | tf_op jit(solution)/shard_map/ppermute | solution.py:18
  585.9 543.3 %reduce-scatter.5.cloned.1.call-start = ((), (), s32[]{:S(2)}) async-start(), calls=%async_computation.3 | async-start | bytes 147456 | tf_op jit(solution)/shard_map/reduce_scatter | solution.py:258
  611.4 228.8 %collective-permute-start.12 = (f32[1024,512]{1,0:T(8,128)}, f32[1024,512]{1,0:T(8,128)}, u32[]{:S(2)}, u32[]{:S(2)}) collective-permute-start(f32[1024,512]{1,0:T(8,128)} %pad_maximum_fusion.1), channel_id=1, source_target_pairs={{0,8},{1,9},{2,10},{3,11},{4,12},{5,13},{6,14},{7,15},{8,0},{9,1},... | collective-permute-start | bytes 6291464 | tf_op jit(solution)/shard_map/ppermute | solution.py:18
  724.9 129.5 %collective-permute-start.8 = (f32[1024,512]{1,0:T(8,128)}, f32[1024,512]{1,0:T(8,128)}, u32[]{:S(2)}, u32[]{:S(2)}) collective-permute-start(f32[1024,512]{1,0:T(8,128)} %pad_maximum_fusion), channel_id=1, source_target_pairs={{0,8},{1,9},{2,10},{3,11},{4,12},{5,13},{6,14},{7,15},{8,0},{9,1},... | collective-permute-start | bytes 6291464 | tf_op jit(solution)/shard_map/ppermute | solution.py:18
  852.9 53.4 %collective-permute-start.13 = (f32[1024,512]{1,0:T(8,128)}, f32[1024,512]{1,0:T(8,128)}, u32[]{:S(2)}, u32[]{:S(2)}) collective-permute-start(f32[1024,512]{1,0:T(8,128)} %maximum_add_fusion.4), channel_id=1, source_target_pairs={{0,4},{1,5},{2,6},{3,7},{4,0},{5,1},{6,2},{7,3},{8,12},{9,13},{10,... | collective-permute-start | bytes 6291464 | tf_op jit(solution)/shard_map/ppermute | solution.py:18
  866.7 76.3 %collective-permute-start.9 = (f32[1024,512]{1,0:T(8,128)}, f32[1024,512]{1,0:T(8,128)}, u32[]{:S(2)}, u32[]{:S(2)}) collective-permute-start(f32[1024,512]{1,0:T(8,128)} %maximum_add_fusion), channel_id=1, source_target_pairs={{0,4},{1,5},{2,6},{3,7},{4,0},{5,1},{6,2},{7,3},{8,12},{9,13},{10,... | collective-permute-start | bytes 6291464 | tf_op jit(solution)/shard_map/ppermute | solution.py:18
  919.8 104.9 %collective-permute-start.14 = (f32[1024,512]{1,0:T(8,128)}, f32[1024,512]{1,0:T(8,128)}, u32[]{:S(2)}, u32[]{:S(2)}) collective-permute-start(f32[1024,512]{1,0:T(8,128)} %maximum_add_fusion.5), channel_id=1, source_target_pairs={{0,2},{1,3},{2,0},{3,1},{4,6},{5,7},{6,4},{7,5},{8,10},{9,11},{10,... | collective-permute-start | bytes 6291464 | tf_op jit(solution)/shard_map/ppermute | solution.py:18
  955.8 82.7 %collective-permute-start.10 = (f32[1024,512]{1,0:T(8,128)}, f32[1024,512]{1,0:T(8,128)}, u32[]{:S(2)}, u32[]{:S(2)}) collective-permute-start(f32[1024,512]{1,0:T(8,128)} %maximum_add_fusion.1), channel_id=1, source_target_pairs={{0,2},{1,3},{2,0},{3,1},{4,6},{5,7},{6,4},{7,5},{8,10},{9,11},{10,... | collective-permute-start | bytes 6291464 | tf_op jit(solution)/shard_map/ppermute | solution.py:18
  1037.2 49.1 %collective-permute-start.15 = (f32[1024,512]{1,0:T(8,128)}, f32[1024,512]{1,0:T(8,128)}, u32[]{:S(2)}, u32[]{:S(2)}) collective-permute-start(f32[1024,512]{1,0:T(8,128)} %maximum_add_fusion.6), channel_id=1, source_target_pairs={{0,1},{1,0},{2,3},{3,2},{4,5},{5,4},{6,7},{7,6},{8,9},{9,8},{10,11... | collective-permute-start | bytes 6291464 | tf_op jit(solution)/shard_map/ppermute | solution.py:18
  1048.9 77.1 %collective-permute-start.11 = (f32[1024,512]{1,0:T(8,128)}, f32[1024,512]{1,0:T(8,128)}, u32[]{:S(2)}, u32[]{:S(2)}) collective-permute-start(f32[1024,512]{1,0:T(8,128)} %maximum_add_fusion.2), channel_id=1, source_target_pairs={{0,1},{1,0},{2,3},{3,2},{4,5},{5,4},{6,7},{7,6},{8,9},{9,8},{10,11... | collective-permute-start | bytes 6291464 | tf_op jit(solution)/shard_map/ppermute | solution.py:18
  1068.1 58.0 %copy-start.116 = (f32[1024,128]{1,0:T(8,128)S(1)}, f32[1024,128]{1,0:T(8,128)}, u32[]{:S(2)}) copy-start(f32[1024,128]{1,0:T(8,128)} %copy.1629) | copy-start | bytes 1572868
  1068.1 58.0 %copy-start.117 = (f32[1024,128]{1,0:T(8,128)S(1)}, f32[1024,128]{1,0:T(8,128)}, u32[]{:S(2)}) copy-start(f32[1024,128]{1,0:T(8,128)} %copy.1630) | copy-start | bytes 1572868
  1068.1 58.0 %copy-start.118 = (f32[1024,128]{1,0:T(8,128)S(1)}, f32[1024,128]{1,0:T(8,128)}, u32[]{:S(2)}) copy-start(f32[1024,128]{1,0:T(8,128)} %copy.1631) | copy-start | bytes 1572868
  (320 other events, 1833.5 us)
Sparse Core Ops, SparseCore 0:
  586.0 102.9 reduce-scatter.2
  1061.8 29.5 reduce-scatter.4
where the time goes:
time: 1150 us; the launch traced here: 1140 us
  local copies, waits for them, and re-layouts  490 us (43%)
  matrix products  309 us (27%)
  other arithmetic  219 us (19%)
  waiting for transfers between devices  73.4 us (6%)
  starting transfers between devices  27.4 us (2%)
  between operations  18.6 us (2%)
    ppermute x16, waiting for transfers between devices, partner(): return lax.ppermute(value, axis, pairs)  73.4 us
    slice x54, local copies, waits for them, and re-layouts, columns_of(): return matrix[:, first_col:first_col + group_width]  67.4 us
    dot_general x16, matrix products, attend_forward(): jnp.einsum('hpr,rhd->phd', exponent.astype(jnp.bfloat16), split_heads(val...  60.6 us
    dot_general x16, matrix products, attend_backward(): jnp.einsum('phd,rhd->hpr', grad_heads, value_heads, preferred_element_typ...  60.6 us
    reshape x32, local copies, waits for them, and re-layouts, widened(): return jnp.repeat(stat.T, head_dim, axis=1)  55.4 us
    dot_general x16, matrix products, attend_backward(): jnp.einsum('hpr,phd->rhd', exponent.astype(jnp.bfloat16), grad_heads, pre...  52.3 us
    reduce_sum x16, other arithmetic, attend_forward(): totals = jnp.sum(exponent, axis=2)  47.6 us
    dot_general x16, matrix products, head_scores(): jnp.einsum('phd,rhd->hpr', query_heads, key_heads, preferred_element_type...  46.6 us
  transfers between devices with their start and end apart: 18, of which 3 were waited for; matrix products, arithmetic and copies ran while one was open for 70% of the time, Pallas kernels for 0%

commit v1 on v0

v1 whole, which is shorter than its diff:
```python
import functools

import jax
import jax.numpy as jnp
from jax import lax
from jax.experimental import pallas as pl
from jax.experimental.pallas import tpu as pltpu
from jax.sharding import PartitionSpec as P

F32=jnp.float32; BF=jnp.bfloat16
KEYS=1024; SLAB=128; TW=256
NT=(((1,),(1,)),((),()))
NN=(((1,),(0,)),((),()))
LOG2E=1.4426950408889634
TILES=23
BLK=[(0,0,8),(1,8,8),(2,16,4),(3,20,2),(4,22,1)]

def dot(a,b,dims=NN):
    return lax.dot_general(a,b,dims,preferred_element_type=F32)

def kernel(q_ref, ga_ref, kv0,kv1,kv2,kv3,kv4, attn_ref, dq_ref, g0,g1,g2,g3,g4,
           kk,va,kT,vT,qw,qk,gw,gk,p_ref,ds_ref,w_ref,st_ref,s_ref,dqt_ref):
    kvs=[kv0,kv1,kv2,kv3,kv4]
    gouts=[g0,g1,g2,g3,g4]
    ones3=(lax.broadcasted_iota(jnp.int32,(KEYS,64),1)<3).astype(F32).astype(BF)
    for b in range(5):
        k=kvs[b][:,0:128]; v=kvs[b][:,128:256]
        k0=k[:,0:64]; k1=k[:,64:128]; v0=v[:,0:64]; v1=v[:,64:128]
        kk[b]=jnp.concatenate([k0,k0,k1,k1],1)
        va[b]=jnp.concatenate([v0,ones3,v1,ones3],1)
        kT[b]=k.T
        vT[b,0:128]=v.T
        vT[b,128:144]=(lax.broadcasted_iota(jnp.int32,(16,KEYS),0)==0).astype(F32).astype(BF)
    zero=jnp.zeros((64,SLAB),BF)
    def put_q(t,q):
        qs=q.astype(F32)*(0.125*LOG2E)
        hi=qs.astype(BF); lo=(qs-hi.astype(F32)).astype(BF)
        qw[t,0:64,0:128]=hi[0:64]; qw[t,64:128,0:128]=lo[0:64]
        qw[t,128:192,0:128]=zero; qw[t,192:256,0:128]=zero
        qw[t,0:64,128:256]=zero; qw[t,64:128,128:256]=zero
        qw[t,128:192,128:256]=hi[64:128]; qw[t,192:256,128:256]=lo[64:128]
        qq=(q.astype(F32)*0.125).astype(BF)
        qk[0:64,t*TW:t*TW+128]=qq[0:64]; qk[64:128,t*TW:t*TW+128]=zero
        qk[0:64,t*TW+128:t*TW+256]=zero; qk[64:128,t*TW+128:t*TW+256]=qq[64:128]
    level=[q_ref[:,j*SLAB:(j+1)*SLAB] for j in range(8)]
    for j in range(8):
        put_q(j,level[j]);
    for l,first in ((1,16),(2,20),(3,22)):
        level=[(0.5*(level[2*c].astype(F32)+level[2*c+1].astype(F32))).astype(BF) for c in range(len(level)//2)]
        for c,x in enumerate(level): put_q(first+c,x)

    def fwd(t,b,tq):
        s=dot(kk[b],qw[tq])
        s_ref[...]=s
        m=jnp.max(s_ref[...],axis=0,keepdims=True)
        p=jnp.exp2(s_ref[...]-m).astype(BF)
        off=pl.multiple_of(t*TW,TW)
        p_ref[:,pl.ds(off,TW)]=p
        w=dot(vT[b],p)
        w_ref[t]=jnp.concatenate([w[0:64,0:128],w[64:128,128:256]],1)
        st_ref[t,0:1]=m
        st_ref[t,1:2]=w[128:129]
    for b,first,n in BLK:
        def body(i,c,b=b,first=first):
            fwd(first+i,b,i if b==1 else first+i)
            return c
        lax.fori_loop(0,n,body,0)

    gl=[None]*TILES; gs=[None]*TILES
    def acc(lst,i,x): lst[i]=x if lst[i] is None else lst[i]+x
    for j in range(8):
        ts=[j,8+j,16+j//2,20+j//4,22]
        ms=[st_ref[t,0:1] for t in ts]; tt=[st_ref[t,1:2] for t in ts]
        mx=functools.reduce(jnp.maximum,ms)
        fs=[jnp.exp2(m-mx)*w for m,w in zip(ms,(1.,1.,2.,4.,8.))]
        tot=functools.reduce(jnp.add,[f*x for f,x in zip(fs,tt)])
        inv=1.0/tot
        sh=[f*inv for f in fs]
        at=functools.reduce(jnp.add,[s*w_ref[t] for s,t in zip(sh,ts)])
        atb=at.astype(BF)
        attn_ref[0:64,j*SLAB:(j+1)*SLAB]=atb[:,0:128]
        attn_ref[64:128,j*SLAB:(j+1)*SLAB]=atb[:,128:256]
        ga=jnp.concatenate([ga_ref[0:64,j*SLAB:(j+1)*SLAB],ga_ref[64:128,j*SLAB:(j+1)*SLAB]],1).astype(F32)
        delta=jnp.sum(ga*atb.astype(F32),axis=0,keepdims=True)
        for s,t in zip(sh,ts):
            acc(gl,t,s*ga); acc(gs,t,s*delta)
    z64=jnp.zeros((64,SLAB),BF); z48=jnp.zeros((48,SLAB),BF)
    for t in range(TILES):
        g=gl[t].astype(BF)
        n=-gs[t]
        hi=n.astype(BF).astype(F32); r=n-hi; mid=r.astype(BF).astype(F32); lo=r-mid
        row=lax.broadcasted_iota(jnp.int32,(16,TW),0)
        gsb=jnp.where(row==0,hi,jnp.where(row==1,mid,jnp.where(row==2,lo,0.0))).astype(BF)
        gw[t,0:64,0:128]=g[:,0:128]; gw[t,64:80,0:128]=gsb[:,0:128]; gw[t,80:128,0:128]=z48
        gw[t,128:192,0:128]=z64; gw[t,192:256,0:128]=z64
        gw[t,0:64,128:256]=z64; gw[t,64:128,128:256]=z64
        gw[t,128:192,128:256]=g[:,128:256]; gw[t,192:208,128:256]=gsb[:,128:256]; gw[t,208:256,128:256]=z48
        gk[0:64,t*TW:t*TW+128]=g[:,0:128]; gk[64:128,t*TW:t*TW+128]=z64
        gk[0:64,t*TW+128:t*TW+256]=z64; gk[64:128,t*TW+128:t*TW+256]=g[:,128:256]

    for b,first,n in BLK:
        qoff=0 if b==1 else first
        def body(i,c,b=b,first=first):
            t=first+i
            off=pl.multiple_of(t*TW,TW)
            dp=dot(va[b],gw[t])
            ds=(p_ref[:,pl.ds(off,TW)].astype(F32)*dp).astype(BF)
            ds_ref[:,pl.ds(pl.multiple_of(i*TW,TW),TW)]=ds
            dq=dot(kT[b],ds)
            dqt_ref[t]=jnp.concatenate([dq[0:64,0:128],dq[64:128,128:256]],1)
            return c
        lax.fori_loop(0,n,body,0)
        def body2(i,c,b=b,first=first,n=n,qoff=qoff):
            rows=pl.ds(pl.multiple_of(i*256,256),256)
            dk=dot(ds_ref[rows,0:n*TW],qk[:,qoff*TW:(qoff+n)*TW],NT)
            dv=dot(p_ref[rows,first*TW:(first+n)*TW],gk[:,first*TW:(first+n)*TW],NT)
            gouts[b][rows,0:128]=dk.astype(gouts[b].dtype)
            gouts[b][rows,128:256]=dv.astype(gouts[b].dtype)
            return c
        lax.fori_loop(0,4,body2,0)
    for j in range(8):
        d=0.125*(dqt_ref[j]+dqt_ref[8+j]+0.5*dqt_ref[16+j//2]+0.25*dqt_ref[20+j//4]+0.125*dqt_ref[22])
        d=d.astype(BF)
        dq_ref[0:64,j*SLAB:(j+1)*SLAB]=d[:,0:128]
        dq_ref[64:128,j*SLAB:(j+1)*SLAB]=d[:,128:256]

def main(g,qT,gaT,kvs,gdt=F32):
    spec=lambda: pl.BlockSpec((KEYS,256),lambda i:(0,0))
    colspec=pl.BlockSpec((128,KEYS),lambda i:(g,0))
    return pl.pallas_call(kernel,grid=(1,),
        in_specs=[colspec,colspec]+[spec()]*5,
        out_specs=[pl.BlockSpec((128,KEYS),lambda i:(0,0))]*2+[spec()]*5,
        out_shape=[jax.ShapeDtypeStruct((128,KEYS),BF)]*2+[jax.ShapeDtypeStruct((KEYS,256),F32)]+[jax.ShapeDtypeStruct((KEYS,256),gdt)]*4,
        scratch_shapes=[pltpu.VMEM((5,KEYS,256),BF),pltpu.VMEM((5,KEYS,256),BF),pltpu.VMEM((5,128,KEYS),BF),pltpu.VMEM((5,144,KEYS),BF),
          pltpu.VMEM((TILES,256,TW),BF),pltpu.VMEM((128,TILES*TW),BF),pltpu.VMEM((TILES,256,TW),BF),pltpu.VMEM((128,TILES*TW),BF),
          pltpu.VMEM((KEYS,TILES*TW),BF),pltpu.VMEM((KEYS,8*TW),BF),pltpu.VMEM((TILES,64,TW),F32),pltpu.VMEM((TILES,8,TW),F32),
          pltpu.VMEM((KEYS,TW),F32),pltpu.VMEM((TILES,64,TW),F32)],
        compiler_params=pltpu.CompilerParams(vmem_limit_bytes=56*2**20),
        name="group")(qT,gaT,*kvs)


GROUPS = 4
MASKS = (1, 3, 4, 12)


def to_slabs(src, tmp, width):
    tmp[...] = src[...].astype(F32)
    return [tmp[pl.ds(b, SLAB, stride=8), 0:width] for b in range(8)]


def keys_kernel(k_ref, v_ref, o0, o1, o2, o3, tmp):
    outs = (o0, o1, o2, o3)
    for part, src in enumerate((k_ref, v_ref)):
        for g in range(GROUPS):
            tmp[...] = src[:, g * 128 : (g + 1) * 128].astype(F32)
            for b in range(8):
                outs[g][b * SLAB : (b + 1) * SLAB, part * 128 : (part + 1) * 128] = tmp[
                    pl.ds(b, SLAB, stride=8), :
                ].astype(BF)


def prep_keys(k, v):
    return pl.pallas_call(
        keys_kernel,
        out_shape=[jax.ShapeDtypeStruct((KEYS, 256), BF)] * GROUPS,
        scratch_shapes=[pltpu.VMEM((KEYS, 128), F32)],
        compiler_params=pltpu.CompilerParams(vmem_limit_bytes=32 * 2**20),
        name="prep_keys",
    )(k, v)


def rows_kernel(q_ref, go_ref, w_ref, qT_ref, gaT_ref, gp_ref, tmp):
    for g in range(GROUPS):
        tmp[...] = q_ref[:, g * 128 : (g + 1) * 128].astype(F32)
        for b in range(8):
            x = tmp[pl.ds(b, SLAB, stride=8), :]
            qT_ref[g * 128 : (g + 1) * 128, b * SLAB : (b + 1) * SLAB] = x.T.astype(BF)
    for c in range(8):
        tmp[...] = go_ref[:, c * 128 : (c + 1) * 128].astype(F32)
        for b in range(8):
            gp_ref[b * SLAB : (b + 1) * SLAB, c * 128 : (c + 1) * 128] = tmp[
                pl.ds(b, SLAB, stride=8), :
            ].astype(BF)
    for c in range(4):
        rows = pl.ds(c * 256, 256)
        gaT_ref[:, c * 256 : (c + 1) * 256] = dot(w_ref[...], gp_ref[rows, :], NT).astype(BF)


def prep_rows(q, go, w):
    return pl.pallas_call(
        rows_kernel,
        out_shape=[
            jax.ShapeDtypeStruct((512, KEYS), BF),
            jax.ShapeDtypeStruct((512, KEYS), BF),
            jax.ShapeDtypeStruct((KEYS, 1024), BF),
        ],
        scratch_shapes=[pltpu.VMEM((KEYS, 128), F32)],
        compiler_params=pltpu.CompilerParams(vmem_limit_bytes=40 * 2**20),
        name="prep_rows",
    )(q, go, w)


def project_kernel(a0, a1, a2, a3, gp_ref, w_ref, out_ref, gw_ref, at, tmp):
    attns = (a0, a1, a2, a3)
    for g in range(GROUPS):
        at[:, g * 128 : (g + 1) * 128] = attns[g][...].T
        gw_ref[g * 128 : (g + 1) * 128, :] = dot(attns[g][...], gp_ref[...])
    for c in range(8):
        for b in range(8):
            tmp[pl.ds(b, SLAB, stride=8), :] = dot(
                at[b * SLAB : (b + 1) * SLAB, :], w_ref[:, c * 128 : (c + 1) * 128]
            )
        out_ref[:, c * 128 : (c + 1) * 128] = tmp[...].astype(BF)


def project(attns, gp, w):
    return pl.pallas_call(
        project_kernel,
        out_shape=[
            jax.ShapeDtypeStruct((KEYS, 1024), BF),
            jax.ShapeDtypeStruct((512, 1024), F32),
        ],
        scratch_shapes=[pltpu.VMEM((KEYS, 512), BF), pltpu.VMEM((KEYS, 128), F32)],
        compiler_params=pltpu.CompilerParams(vmem_limit_bytes=40 * 2**20),
        name="project",
    )(*attns, gp, w)


def queries_kernel(d0, d1, d2, d3, out_ref, tmp):
    for g, d in enumerate((d0, d1, d2, d3)):
        for b in range(8):
            tmp[pl.ds(b, SLAB, stride=8), :] = d[:, b * SLAB : (b + 1) * SLAB].astype(F32).T
        out_ref[:, g * 128 : (g + 1) * 128] = tmp[...].astype(BF)


def finish_queries(dqs):
    return pl.pallas_call(
        queries_kernel,
        out_shape=jax.ShapeDtypeStruct((KEYS, 512), BF),
        scratch_shapes=[pltpu.VMEM((KEYS, 128), F32)],
        compiler_params=pltpu.CompilerParams(vmem_limit_bytes=32 * 2**20),
        name="finish_queries",
    )(*dqs)


def finish_kernel(*refs):
    parts, (dk_ref, dv_ref, tmp) = refs[: 3 * GROUPS], refs[3 * GROUPS :]
    for g in range(GROUPS):
        own, kept, got = parts[3 * g : 3 * g + 3]
        for part, out in enumerate((dk_ref, dv_ref)):
            cols = slice(part * 128, (part + 1) * 128)
            for b in range(8):
                rows = slice(b * SLAB, (b + 1) * SLAB)
                half = slice(b // 2 * SLAB, (b // 2 + 1) * SLAB)
                tmp[pl.ds(b, SLAB, stride=8), :] = (
                    own[rows, cols] + 0.5 * kept[half, cols] + got[rows, cols].astype(F32)
                )
            out[:, g * 128 : (g + 1) * 128] = tmp[...].astype(BF)


def finish_keys(parts):
    return pl.pallas_call(
        finish_kernel,
        out_shape=[jax.ShapeDtypeStruct((KEYS, 512), BF)] * 2,
        scratch_shapes=[pltpu.VMEM((KEYS, 128), F32)],
        compiler_params=pltpu.CompilerParams(vmem_limit_bytes=40 * 2**20),
        name="finish_keys",
    )(*[x for part in parts for x in part])


def partner(value, level):
    mask = MASKS[level]
    pairs = [(source, source ^ mask) for source in range(lax.axis_size("ctx"))]
    return lax.ppermute(value, "ctx", pairs)


def pool(x):
    y = x.astype(F32).reshape(4, 2, SLAB, 256)
    return (0.5 * (y[:, 0] + y[:, 1])).astype(BF).reshape(512, 256)


def spread(x):
    y = jnp.broadcast_to((0.5 * x).reshape(4, 1, SLAB, 256), (4, 2, SLAB, 256))
    return y.reshape(KEYS, 256)


def on_device(queries, key_states, value_states, grad_out, out_weight):
    held = list(prep_keys(key_states[0], value_states[0]))
    kvs = [[h] for h in held]
    for level in range(4):
        far = [partner(h, level) for h in held]
        for g in range(GROUPS):
            kvs[g].append(far[g])
        if level < 3:
            held = [jnp.concatenate([pool(h), pool(f)], 0) for h, f in zip(held, far)]
    qT, gaT, gp = prep_rows(queries[0], grad_out[0], out_weight)
    attns, dqs, parts = [], [], []
    for g in range(GROUPS):
        attn, dq, own, f0, f1, f2, f3 = main(g, qT, gaT, kvs[g], BF)
        attns.append(attn)
        dqs.append(dq)
        pending = partner(f3, 3).astype(F32)
        for level, f in ((2, f2), (1, f1), (0, f0)):
            outgoing = (f.astype(F32) + spread(pending[512:])).astype(BF)
            incoming = partner(outgoing, level)
            kept = pending[:512]
            if level:
                pending = spread(kept) + incoming.astype(F32)
        parts.append((own, kept, incoming))
    outputs, weight_part = project(attns, gp, out_weight)
    grad_queries = finish_queries(dqs)
    grad_keys, grad_values = finish_keys(parts)
    rows = lax.psum_scatter(weight_part, "ctx", scatter_dimension=0, tiled=True)
    grad_weight = lax.psum_scatter(rows, "rep", scatter_dimension=1, tiled=True)
    return outputs[None], grad_queries[None], grad_keys[None], grad_values[None], grad_weight


def solution(mesh):
    rows = P("rep", "ctx", None)
    return jax.shard_map(
        on_device,
        mesh=mesh,
        in_specs=(rows, rows, rows, rows, P()),
        out_specs=(rows, rows, rows, rows, P("ctx", "rep")),
        check_vma=False,
    )
```

time: 1150 us -> 467 us (0.41)
  local copies, waits for them, and re-layouts: 490 us -> 22.7 us
  matrix products: 309 us -> 0 us
  other arithmetic: 219 us -> 11.4 us
  Pallas kernels: 0 us -> 203 us
  waiting for transfers between devices: 73.4 us -> 157 us
  starting transfers between devices: 27.4 us -> 49.6 us
    dot_general x103 -> x0, matrix products: 309 us -> none  [the longest x16 60.6 us: attend_forward(): jnp.einsum('hpr,rhd->phd', exponent.astype(jnp.bfloat16), split_heads(val...]
    pallas_call x0 -> x9, Pallas kernels: none -> 203 us  [the longest x4 187 us: main(): pl.pallas_call(kernel, grid=(1,), in_specs=[colspec, colspec] + [spec()]...]
    reshape x110 -> x0, local copies, waits for them, and re-layouts: 180 us -> none  [the longest x32 55.4 us: widened(): return jnp.repeat(stat.T, head_dim, axis=1)]
    slice x78 -> x0, local copies, waits for them, and re-layouts: 108 us -> none  [the longest x54 67.4 us: columns_of(): return matrix[:, first_col:first_col + group_width]]
    reduce_sum x37 -> x0, other arithmetic: 74.5 us -> none  [the longest x16 47.6 us: attend_forward(): totals = jnp.sum(exponent, axis=2)]
    ppermute x16 -> x32, waiting for transfers between devices: 73.4 us -> 147 us  [partner(): return lax.ppermute(value, 'ctx', pairs)]
    broadcast_in_dim x84 -> x0, local copies, waits for them, and re-layouts: 72.7 us -> none  [the longest x32 25.2 us: widened(): return jnp.repeat(stat.T, head_dim, axis=1)]
    convert_element_type x20 -> x48, other arithmetic: 62.8 us -> 7.28 us  [the longest x12 4.45 us: on_device(): outgoing = (f.astype(F32) + spread(pending[512:])).astype(BF)]
  transfers between devices with their start and end apart: 18 -> 34, of which waited for: 3 -> 21; matrix products, arithmetic and copies ran while one was open for 70% -> 2% of each run, Pallas kernels for 0% -> 33%
where the time goes in v1:
time: 467 us; the launch traced here: 459 us
  Pallas kernels  203 us (43%)
  waiting for transfers between devices  157 us (34%)
  starting transfers between devices  49.6 us (11%)
  local copies, waits for them, and re-layouts  22.7 us (5%)
  between operations  15.6 us (3%)
  other arithmetic  11.4 us (2%)
    pallas_call x4, Pallas kernels, main(): pl.pallas_call(kernel, grid=(1,), in_specs=[colspec, colspec] + [spec()]...  187 us
    ppermute x32, waiting for transfers between devices, partner(): return lax.ppermute(value, 'ctx', pairs)  147 us
    ppermute x32, starting transfers between devices, partner(): return lax.ppermute(value, 'ctx', pairs)  49.5 us
    unnamed x110, local copies, waits for them, and re-layouts  22.7 us
    reduce_scatter x1, waiting for transfers between devices, on_device(): grad_weight = lax.psum_scatter(rows, 'rep', scatter_dimension=1, tiled=True)  9.7 us
  transfers between devices with their start and end apart: 34, of which 21 were waited for; matrix products, arithmetic and copies ran while one was open for 2% of the time, Pallas kernels for 33%

profile of v1, /device:TPU:0, one launch (start us, length us, event | category | flops | bytes accessed | tf_op | source)
XLA Modules:
  0.0 458.9 jit_solution(286895039777257894)
XLA Ops:
  15.7 9.9 %collective-permute-done.12.kv1 = bf16[1024,256]{1,0:T(8,128)(2,1)S(1)} collective-permute-done((bf16[1024,256]{1,0:T(8,128)(2,1)S(1)}, bf16[1024,256]{1,0:T(8,128)(2,1)S(1)}, u32[]{:S(2)}, u32[]{:S(2)}) %collective-permute-start.12) | collective-permute-done | bytes 524320 | tf_op jit(solution)/shard_map/ppermute | solution.py:274
  30.2 6.7 %collective-permute-done.8.kv1 = bf16[1024,256]{1,0:T(8,128)(2,1)S(1)} collective-permute-done((bf16[1024,256]{1,0:T(8,128)(2,1)S(1)}, bf16[1024,256]{1,0:T(8,128)(2,1)S(1)}, u32[]{:S(2)}, u32[]{:S(2)}) %collective-permute-start.8) | collective-permute-done | bytes 524320 | tf_op jit(solution)/shard_map/ppermute | solution.py:274
  41.3 6.8 %collective-permute-done.4.kv1 = bf16[1024,256]{1,0:T(8,128)(2,1)S(1)} collective-permute-done((bf16[1024,256]{1,0:T(8,128)(2,1)S(1)}, bf16[1024,256]{1,0:T(8,128)(2,1)S(1)}, u32[]{:S(2)}, u32[]{:S(2)}) %collective-permute-start.4) | collective-permute-done | bytes 524320 | tf_op jit(solution)/shard_map/ppermute | solution.py:274
  53.2 5.2 %collective-permute-done.kv1 = bf16[1024,256]{1,0:T(8,128)(2,1)S(1)} collective-permute-done((bf16[1024,256]{1,0:T(8,128)(2,1)S(1)}, bf16[1024,256]{1,0:T(8,128)(2,1)S(1)}, u32[]{:S(2)}, u32[]{:S(2)}) %collective-permute-start) | collective-permute-done | bytes 524320 | tf_op jit(solution)/shard_map/ppermute | solution.py:274
  68.7 5.5 %collective-permute-done.1.kv2 = bf16[1024,256]{1,0:T(8,128)(2,1)S(1)} collective-permute-done((bf16[1024,256]{1,0:T(8,128)(2,1)S(1)}, bf16[1024,256]{1,0:T(8,128)(2,1)S(1)}, u32[]{:S(2)}, u32[]{:S(2)}) %collective-permute-start.1) | collective-permute-done | bytes 524320 | tf_op jit(solution)/shard_map/ppermute | solution.py:274
  81.9 7.9 %collective-permute-done.10.kv3 = bf16[1024,256]{1,0:T(8,128)(2,1)S(1)} collective-permute-done((bf16[1024,256]{1,0:T(8,128)(2,1)S(1)}, bf16[1024,256]{1,0:T(8,128)(2,1)S(1)}, u32[]{:S(2)}, u32[]{:S(2)}) %collective-permute-start.10) | collective-permute-done | bytes 524320 | tf_op jit(solution)/shard_map/ppermute | solution.py:274
  93.9 7.2 %collective-permute-done.6.kv3 = bf16[1024,256]{1,0:T(8,128)(2,1)S(1)} collective-permute-done((bf16[1024,256]{1,0:T(8,128)(2,1)S(1)}, bf16[1024,256]{1,0:T(8,128)(2,1)S(1)}, u32[]{:S(2)}, u32[]{:S(2)}) %collective-permute-start.6) | collective-permute-done | bytes 524320 | tf_op jit(solution)/shard_map/ppermute | solution.py:274
  104.4 5.5 %collective-permute-done.2.kv3 = bf16[1024,256]{1,0:T(8,128)(2,1)S(1)} collective-permute-done((bf16[1024,256]{1,0:T(8,128)(2,1)S(1)}, bf16[1024,256]{1,0:T(8,128)(2,1)S(1)}, u32[]{:S(2)}, u32[]{:S(2)}) %collective-permute-start.2) | collective-permute-done | bytes 524320 | tf_op jit(solution)/shard_map/ppermute | solution.py:274
  119.3 44.7 %group.7 = (bf16[128,1024]{1,0:T(8,128)(2,1)}, bf16[128,1024]{1,0:T(8,128)(2,1)}, f32[1024,256]{1,0:T(8,128)}, bf16[1024,256]{1,0:T(8,128)(2,1)}, bf16[1024,256]...) custom-call(bf16[512,1024]{1,0:T(8,128)(2,1)} %copy-done, bf16[512,1024]{1,0:T(8,128)(2,1)} %copy-done.1, ...), custom_call_target="tpu_custom_call" | custom-call | tf_op jit(solution)/shard_map/group/pallas_call | solution.py:130
  164.9 53.0 %group.6 = (bf16[128,1024]{1,0:T(8,128)(2,1)}, bf16[128,1024]{1,0:T(8,128)(2,1)}, f32[1024,256]{1,0:T(8,128)}, bf16[1024,256]{1,0:T(8,128)(2,1)}, bf16[1024,256]...) custom-call(bf16[512,1024]{1,0:T(8,128)(2,1)} %copy-done, bf16[512,1024]{1,0:T(8,128)(2,1)} %copy-done.1, ...), custom_call_target="tpu_custom_call" | custom-call | tf_op jit(solution)/shard_map/group/pallas_call | solution.py:130
  218.6 44.7 %group.5 = (bf16[128,1024]{1,0:T(8,128)(2,1)}, bf16[128,1024]{1,0:T(8,128)(2,1)}, f32[1024,256]{1,0:T(8,128)}, bf16[1024,256]{1,0:T(8,128)(2,1)}, bf16[1024,256]...) custom-call(bf16[512,1024]{1,0:T(8,128)(2,1)} %copy-done, bf16[512,1024]{1,0:T(8,128)(2,1)} %copy-done.1, ...), custom_call_target="tpu_custom_call" | custom-call | tf_op jit(solution)/shard_map/group/pallas_call | solution.py:130
  264.2 44.6 %group.4 = (bf16[128,1024]{1,0:T(8,128)(2,1)}, bf16[128,1024]{1,0:T(8,128)(2,1)}, f32[1024,256]{1,0:T(8,128)}, bf16[1024,256]{1,0:T(8,128)(2,1)}, bf16[1024,256]...) custom-call(bf16[512,1024]{1,0:T(8,128)(2,1)} %copy-done, bf16[512,1024]{1,0:T(8,128)(2,1)} %copy-done.1, ...), custom_call_target="tpu_custom_call" | custom-call | tf_op jit(solution)/shard_map/group/pallas_call | solution.py:130
  309.8 6.0 %project.1 = (bf16[1024,1024]{1,0:T(8,128)(2,1)}, f32[512,1024]{1,0:T(8,128)}) custom-call(bf16[128,1024]{1,0:T(8,128)(2,1)S(1)} %copy-done.18, bf16[128,1024]{1,0:T(8,128)(2,1)S(1)} %copy-done.17, bf16[128,1024]{1,0:T(8,128)(2,1)S(1)} %copy-done.16, bf16[128,1024]{1,0:T(8,128)(2,1)S(1)} %copy-done.15, bf16[1024,1024]{1,0:T(8,128)(2,1)S(1)} %get-tuple-element.54.gp_ref, ...), custom_call_target="tpu_custom_call" | custom-call | tf_op jit(solution)/shard_map/project/pallas_call | solution.py:217
  323.2 11.7 %collective-permute-done.28 = bf16[1024,256]{1,0:T(8,128)(2,1)S(1)} collective-permute-done((bf16[1024,256]{1,0:T(8,128)(2,1)S(1)}, bf16[1024,256]{1,0:T(8,128)(2,1)S(1)}, u32[]{:S(2)}, u32[]{:S(2)}) %collective-permute-start.28) | collective-permute-done | bytes 524320 | tf_op jit(solution)/shard_map/ppermute | solution.py:274
  335.3 13.8 %collective-permute-done.24 = bf16[1024,256]{1,0:T(8,128)(2,1)S(1)} collective-permute-done((bf16[1024,256]{1,0:T(8,128)(2,1)S(1)}, bf16[1024,256]{1,0:T(8,128)(2,1)S(1)}, u32[]{:S(2)}, u32[]{:S(2)}) %collective-permute-start.24) | collective-permute-done | bytes 524320 | tf_op jit(solution)/shard_map/ppermute | solution.py:274
  349.5 13.6 %collective-permute-done.20 = bf16[1024,256]{1,0:T(8,128)(2,1)S(1)} collective-permute-done((bf16[1024,256]{1,0:T(8,128)(2,1)S(1)}, bf16[1024,256]{1,0:T(8,128)(2,1)S(1)}, u32[]{:S(2)}, u32[]{:S(2)}) %collective-permute-start.20) | collective-permute-done | bytes 524320 | tf_op jit(solution)/shard_map/ppermute | solution.py:274
  363.6 7.8 %collective-permute-done.16 = bf16[1024,256]{1,0:T(8,128)(2,1)S(1)} collective-permute-done((bf16[1024,256]{1,0:T(8,128)(2,1)S(1)}, bf16[1024,256]{1,0:T(8,128)(2,1)S(1)}, u32[]{:S(2)}, u32[]{:S(2)}) %collective-permute-start.16) | collective-permute-done | bytes 524320 | tf_op jit(solution)/shard_map/ppermute | solution.py:274
  379.3 6.3 %collective-permute-done.17 = bf16[1024,256]{1,0:T(8,128)(2,1)S(1)} collective-permute-done((bf16[1024,256]{1,0:T(8,128)(2,1)S(1)}, bf16[1024,256]{1,0:T(8,128)(2,1)S(1)}, u32[]{:S(2)}, u32[]{:S(2)}) %collective-permute-start.17) | collective-permute-done | bytes 524320 | tf_op jit(solution)/shard_map/ppermute | solution.py:274
  386.8 4.4 collective-permute-done.30
  393.2 9.3 %collective-permute-done.26 = bf16[1024,256]{1,0:T(8,128)(2,1)S(1)} collective-permute-done((bf16[1024,256]{1,0:T(8,128)(2,1)S(1)}, bf16[1024,256]{1,0:T(8,128)(2,1)S(1)}, u32[]{:S(2)}, u32[]{:S(2)}) %collective-permute-start.26) | collective-permute-done | bytes 524320 | tf_op jit(solution)/shard_map/ppermute | solution.py:274
  404.4 9.3 %collective-permute-done.22 = bf16[1024,256]{1,0:T(8,128)(2,1)S(1)} collective-permute-done((bf16[1024,256]{1,0:T(8,128)(2,1)S(1)}, bf16[1024,256]{1,0:T(8,128)(2,1)S(1)}, u32[]{:S(2)}, u32[]{:S(2)}) %collective-permute-start.22) | collective-permute-done | bytes 524320 | tf_op jit(solution)/shard_map/ppermute | solution.py:274
  415.6 4.7 %collective-permute-done.18 = bf16[1024,256]{1,0:T(8,128)(2,1)S(1)} collective-permute-done((bf16[1024,256]{1,0:T(8,128)(2,1)S(1)}, bf16[1024,256]{1,0:T(8,128)(2,1)S(1)}, u32[]{:S(2)}, u32[]{:S(2)}) %collective-permute-start.18) | collective-permute-done | bytes 524320 | tf_op jit(solution)/shard_map/ppermute | solution.py:274
  429.6 6.8 %collective-permute-done.19.refs_2_ = bf16[1024,256]{1,0:T(8,128)(2,1)} collective-permute-done((bf16[1024,256]{1,0:T(8,128)(2,1)}, bf16[1024,256]{1,0:T(8,128)(2,1)}, u32[]{:S(2)}, u32[]{:S(2)}) %collective-permute-start.19) | collective-permute-done | bytes 524320 | tf_op jit(solution)/shard_map/ppermute | solution.py:274
  442.0 9.7 %reduce-scatter.5.cloned.1.call-done = f32[32,128]{1,0:T(8,128)} async-done(((f32[32,1024]{1,0:T(8,128)}), f32[32,128]{1,0:T(8,128)}) %reduce-scatter.5.cloned.1.call-update) | async-done | bytes 16400 | tf_op jit(solution)/shard_map/reduce_scatter | solution.py:314
  (261 shorter events, 98.2 us)
Async XLA Ops:
  7.2 415.1 %reduce-scatter.3.cloned.1.call-start = ((), (), s32[]{:S(2)}) async-start(), calls=%async_computation.2 | async-start | bytes 2228224 | tf_op jit(solution)/shard_map/reduce_scatter | solution.py:313
  12.9 24.0 %collective-permute-start.8 = (bf16[1024,256]{1,0:T(8,128)(2,1)S(1)}, bf16[1024,256]{1,0:T(8,128)(2,1)S(1)}, u32[]{:S(2)}, u32[]{:S(2)}) collective-permute-start(bf16[1024,256]{1,0:T(8,128)(2,1)S(1)} %get-tuple-element.50.kv0), channel_id=1, source_target_pairs={{0,1},{1,0},{2,3},{3,2},{4,5},{5,4},{6,7},{7,6},{8,9},{9,8},{10,11... | collective-permute-start | bytes 1572872 | tf_op jit(solution)/shard_map/ppermute | solution.py:274
  13.0 35.2 %collective-permute-start.4 = (bf16[1024,256]{1,0:T(8,128)(2,1)S(1)}, bf16[1024,256]{1,0:T(8,128)(2,1)S(1)}, u32[]{:S(2)}, u32[]{:S(2)}) collective-permute-start(bf16[1024,256]{1,0:T(8,128)(2,1)S(1)} %get-tuple-element.48.kv0), channel_id=1, source_target_pairs={{0,1},{1,0},{2,3},{3,2},{4,5},{5,4},{6,7},{7,6},{8,9},{9,8},{10,11... | collective-permute-start | bytes 1572872 | tf_op jit(solution)/shard_map/ppermute | solution.py:274
  14.9 43.6 %collective-permute-start = (bf16[1024,256]{1,0:T(8,128)(2,1)S(1)}, bf16[1024,256]{1,0:T(8,128)(2,1)S(1)}, u32[]{:S(2)}, u32[]{:S(2)}) collective-permute-start(bf16[1024,256]{1,0:T(8,128)(2,1)S(1)} %get-tuple-element.46.kv0), channel_id=1, source_target_pairs={{0,1},{1,0},{2,3},{3,2},{4,5},{5,4},{6,7},{7,6},{8,9},{9,8},{10,11... | collective-permute-start | bytes 1572872 | tf_op jit(solution)/shard_map/ppermute | solution.py:274
  25.9 37.5 %collective-permute-start.13 = (bf16[1024,256]{1,0:T(8,128)(2,1)S(1)}, bf16[1024,256]{1,0:T(8,128)(2,1)S(1)}, u32[]{:S(2)}, u32[]{:S(2)}) collective-permute-start(bf16[1024,256]{1,0:T(8,128)(2,1)S(1)} %pad_maximum_fusion.9), channel_id=1, source_target_pairs={{0,3},{1,2},{2,1},{3,0},{4,7},{5,6},{6,5},{7,4},{8,11},{9,10},{10,... | collective-permute-start | bytes 1572872 | tf_op jit(solution)/shard_map/ppermute | solution.py:274
  37.1 28.3 %collective-permute-start.9 = (bf16[1024,256]{1,0:T(8,128)(2,1)S(1)}, bf16[1024,256]{1,0:T(8,128)(2,1)S(1)}, u32[]{:S(2)}, u32[]{:S(2)}) collective-permute-start(bf16[1024,256]{1,0:T(8,128)(2,1)S(1)} %pad_maximum_fusion.6), channel_id=1, source_target_pairs={{0,3},{1,2},{2,1},{3,0},{4,7},{5,6},{6,5},{7,4},{8,11},{9,10},{10,... | collective-permute-start | bytes 1572872 | tf_op jit(solution)/shard_map/ppermute | solution.py:274
  65.7 24.2 %collective-permute-start.10 = (bf16[1024,256]{1,0:T(8,128)(2,1)S(1)}, bf16[1024,256]{1,0:T(8,128)(2,1)S(1)}, u32[]{:S(2)}, u32[]{:S(2)}) collective-permute-start(bf16[1024,256]{1,0:T(8,128)(2,1)S(1)} %pad_maximum_fusion.7), channel_id=1, source_target_pairs={{0,4},{1,5},{2,6},{3,7},{4,0},{5,1},{6,2},{7,3},{8,12},{9,13},{10,... | collective-permute-start | bytes 1572872 | tf_op jit(solution)/shard_map/ppermute | solution.py:274
  67.0 34.1 %collective-permute-start.6 = (bf16[1024,256]{1,0:T(8,128)(2,1)S(1)}, bf16[1024,256]{1,0:T(8,128)(2,1)S(1)}, u32[]{:S(2)}, u32[]{:S(2)}) collective-permute-start(bf16[1024,256]{1,0:T(8,128)(2,1)S(1)} %pad_maximum_fusion.4), channel_id=1, source_target_pairs={{0,4},{1,5},{2,6},{3,7},{4,0},{5,1},{6,2},{7,3},{8,12},{9,13},{10,... | collective-permute-start | bytes 1572872 | tf_op jit(solution)/shard_map/ppermute | solution.py:274
  75.0 34.9 %collective-permute-start.2 = (bf16[1024,256]{1,0:T(8,128)(2,1)S(1)}, bf16[1024,256]{1,0:T(8,128)(2,1)S(1)}, u32[]{:S(2)}, u32[]{:S(2)}) collective-permute-start(bf16[1024,256]{1,0:T(8,128)(2,1)S(1)} %pad_maximum_fusion.1), channel_id=1, source_target_pairs={{0,4},{1,5},{2,6},{3,7},{4,0},{5,1},{6,2},{7,3},{8,12},{9,13},{10,... | collective-permute-start | bytes 1572872 | tf_op jit(solution)/shard_map/ppermute | solution.py:274
  78.8 39.7 %collective-permute-start.15 = (bf16[1024,256]{1,0:T(8,128)(2,1)S(1)}, bf16[1024,256]{1,0:T(8,128)(2,1)S(1)}, u32[]{:S(2)}, u32[]{:S(2)}) collective-permute-start(bf16[1024,256]{1,0:T(8,128)(2,1)S(1)} %pad_maximum_fusion.11), channel_id=1, source_target_pairs={{0,12},{1,13},{2,14},{3,15},{4,8},{5,9},{6,10},{7,11},{8,4},{9,5},... | collective-permute-start | bytes 1572872 | tf_op jit(solution)/shard_map/ppermute | solution.py:274
  90.9 73.2 %collective-permute-start.11 = (bf16[1024,256]{1,0:T(8,128)(2,1)}, bf16[1024,256]{1,0:T(8,128)(2,1)S(1)}, u32[]{:S(2)}, u32[]{:S(2)}) collective-permute-start(bf16[1024,256]{1,0:T(8,128)(2,1)} %pad_maximum_fusion.8), channel_id=1, source_target_pairs={{0,12},{1,13},{2,14},{3,15},{4,8},{5,9},{6,10},{7,11},{8,4},{9,5},... | collective-permute-start | bytes 1572872 | tf_op jit(solution)/shard_map/ppermute | solution.py:274
  101.3 116.5 %collective-permute-start.7 = (bf16[1024,256]{1,0:T(8,128)(2,1)S(1)}, bf16[1024,256]{1,0:T(8,128)(2,1)S(1)}, u32[]{:S(2)}, u32[]{:S(2)}) collective-permute-start(bf16[1024,256]{1,0:T(8,128)(2,1)S(1)} %pad_maximum_fusion.5), channel_id=1, source_target_pairs={{0,12},{1,13},{2,14},{3,15},{4,8},{5,9},{6,10},{7,11},{8,4},{9,5},... | collective-permute-start | bytes 1572872 | tf_op jit(solution)/shard_map/ppermute | solution.py:274
  110.2 153.2 %collective-permute-start.3 = (bf16[1024,256]{1,0:T(8,128)(2,1)S(1)}, bf16[1024,256]{1,0:T(8,128)(2,1)S(1)}, u32[]{:S(2)}, u32[]{:S(2)}) collective-permute-start(bf16[1024,256]{1,0:T(8,128)(2,1)S(1)} %pad_maximum_fusion.2), channel_id=1, source_target_pairs={{0,12},{1,13},{2,14},{3,15},{4,8},{5,9},{6,10},{7,11},{8,4},{9,5},... | collective-permute-start | bytes 1572872 | tf_op jit(solution)/shard_map/ppermute | solution.py:274
  315.8 135.9 %reduce-scatter.5.cloned.1.call-start = ((), (), s32[]{:S(2)}) async-start(), calls=%async_computation.3 | async-start | bytes 147456 | tf_op jit(solution)/shard_map/reduce_scatter | solution.py:314
  317.0 32.2 %collective-permute-start.24 = (bf16[1024,256]{1,0:T(8,128)(2,1)S(1)}, bf16[1024,256]{1,0:T(8,128)(2,1)S(1)}, u32[]{:S(2)}, u32[]{:S(2)}) collective-permute-start(bf16[1024,256]{1,0:T(8,128)(2,1)S(1)} %copy-done.52), channel_id=1, source_target_pairs={{0,12},{1,13},{2,14},{3,15},{4,8},{5,9},{6,10},{7,11},{8,4},{9,5},... | collective-permute-start | bytes 1572872 | tf_op jit(solution)/shard_map/ppermute | solution.py:274
  320.0 43.2 %collective-permute-start.20 = (bf16[1024,256]{1,0:T(8,128)(2,1)S(1)}, bf16[1024,256]{1,0:T(8,128)(2,1)S(1)}, u32[]{:S(2)}, u32[]{:S(2)}) collective-permute-start(bf16[1024,256]{1,0:T(8,128)(2,1)S(1)} %copy-done.53), channel_id=1, source_target_pairs={{0,12},{1,13},{2,14},{3,15},{4,8},{5,9},{6,10},{7,11},{8,4},{9,5},... | collective-permute-start | bytes 1572872 | tf_op jit(solution)/shard_map/ppermute | solution.py:274
  320.2 51.2 %collective-permute-start.16 = (bf16[1024,256]{1,0:T(8,128)(2,1)S(1)}, bf16[1024,256]{1,0:T(8,128)(2,1)S(1)}, u32[]{:S(2)}, u32[]{:S(2)}) collective-permute-start(bf16[1024,256]{1,0:T(8,128)(2,1)S(1)} %copy-done.54), channel_id=1, source_target_pairs={{0,12},{1,13},{2,14},{3,15},{4,8},{5,9},{6,10},{7,11},{8,4},{9,5},... | collective-permute-start | bytes 1572872 | tf_op jit(solution)/shard_map/ppermute | solution.py:274
  335.2 36.6 %collective-permute-start.29 = (bf16[1024,256]{1,0:T(8,128)(2,1)S(1)}, bf16[1024,256]{1,0:T(8,128)(2,1)S(1)}, u32[]{:S(2)}, u32[]{:S(2)}) collective-permute-start(bf16[1024,256]{1,0:T(8,128)(2,1)S(1)} %fusion.2), channel_id=1, source_target_pairs={{0,4},{1,5},{2,6},{3,7},{4,0},{5,1},{6,2},{7,3},{8,12},{9,13},{10,... | collective-permute-start | bytes 1572872 | tf_op jit(solution)/shard_map/ppermute | solution.py:274
  349.4 24.1 %collective-permute-start.25 = (bf16[1024,256]{1,0:T(8,128)(2,1)S(1)}, bf16[1024,256]{1,0:T(8,128)(2,1)S(1)}, u32[]{:S(2)}, u32[]{:S(2)}) collective-permute-start(bf16[1024,256]{1,0:T(8,128)(2,1)S(1)} %fusion.5), channel_id=1, source_target_pairs={{0,4},{1,5},{2,6},{3,7},{4,0},{5,1},{6,2},{7,3},{8,12},{9,13},{10,... | collective-permute-start | bytes 1572872 | tf_op jit(solution)/shard_map/ppermute | solution.py:274
  374.7 27.7 %collective-permute-start.26 = (bf16[1024,256]{1,0:T(8,128)(2,1)S(1)}, bf16[1024,256]{1,0:T(8,128)(2,1)S(1)}, u32[]{:S(2)}, u32[]{:S(2)}) collective-permute-start(bf16[1024,256]{1,0:T(8,128)(2,1)S(1)} %fusion.4), channel_id=1, source_target_pairs={{0,3},{1,2},{2,1},{3,0},{4,7},{5,6},{6,5},{7,4},{8,11},{9,10},{10,... | collective-permute-start | bytes 1572872 | tf_op jit(solution)/shard_map/ppermute | solution.py:274
  378.6 35.0 %collective-permute-start.22 = (bf16[1024,256]{1,0:T(8,128)(2,1)S(1)}, bf16[1024,256]{1,0:T(8,128)(2,1)S(1)}, u32[]{:S(2)}, u32[]{:S(2)}) collective-permute-start(bf16[1024,256]{1,0:T(8,128)(2,1)S(1)} %fusion.7), channel_id=1, source_target_pairs={{0,3},{1,2},{2,1},{3,0},{4,7},{5,6},{6,5},{7,4},{8,11},{9,10},{10,... | collective-permute-start | bytes 1572872 | tf_op jit(solution)/shard_map/ppermute | solution.py:274
  386.7 33.6 %collective-permute-start.18 = (bf16[1024,256]{1,0:T(8,128)(2,1)S(1)}, bf16[1024,256]{1,0:T(8,128)(2,1)S(1)}, u32[]{:S(2)}, u32[]{:S(2)}) collective-permute-start(bf16[1024,256]{1,0:T(8,128)(2,1)S(1)} %fusion.10), channel_id=1, source_target_pairs={{0,3},{1,2},{2,1},{3,0},{4,7},{5,6},{6,5},{7,4},{8,11},{9,10},{10,... | collective-permute-start | bytes 1572872 | tf_op jit(solution)/shard_map/ppermute | solution.py:274
  393.2 33.7 %collective-permute-start.31 = (bf16[1024,256]{1,0:T(8,128)(2,1)}, bf16[1024,256]{1,0:T(8,128)(2,1)}, u32[]{:S(2)}, u32[]{:S(2)}) collective-permute-start(bf16[1024,256]{1,0:T(8,128)(2,1)} %fusion), channel_id=1, source_target_pairs={{0,1},{1,0},{2,3},{3,2},{4,5},{5,4},{6,7},{7,6},{8,9},{9,8},{10,11... | collective-permute-start | bytes 1572872 | tf_op jit(solution)/shard_map/ppermute | solution.py:274
  404.4 22.4 %collective-permute-start.27 = (bf16[1024,256]{1,0:T(8,128)(2,1)}, bf16[1024,256]{1,0:T(8,128)(2,1)}, u32[]{:S(2)}, u32[]{:S(2)}) collective-permute-start(bf16[1024,256]{1,0:T(8,128)(2,1)} %fusion.3), channel_id=1, source_target_pairs={{0,1},{1,0},{2,3},{3,2},{4,5},{5,4},{6,7},{7,6},{8,9},{9,8},{10,11... | collective-permute-start | bytes 1572872 | tf_op jit(solution)/shard_map/ppermute | solution.py:274
  (65 other events, 539.8 us)
Sparse Core Ops, SparseCore 0:
  315.9 73.6 reduce-scatter.2
  422.4 29.2 reduce-scatter.4
